TPU v7x, 256 devices: a whole 4x4x8 slice. The times are simulated.
256 devices in a mesh: ctx: 32 (over z, x), head: 8 (over y, core).
Axes of the slice: x: 4, y: 4, z: 8, core: 2. Of those that a mesh axis runs over, the one named last changes fastest.
Arguments:
- queries: bfloat16 [3, 64, 12288], P(None, None, 'head'), may hold values from -96 to 96
- key_latent: bfloat16 [8, 65536, 256], P('head', 'ctx'), may hold values from -6 to 6
- value_latent: bfloat16 [8, 65536, 256], P('head', 'ctx'), may hold values from -6 to 6
- key_up: bfloat16 [8, 256, 128], P('head'), may hold values from -0.375 to 0.375
- value_up: bfloat16 [8, 256, 128], P('head'), may hold values from -0.375 to 0.375
- out_weight: bfloat16 [12288, 12288], P('head', 'ctx'), may hold values from -0.0546875 to 0.0546875
- prior_scores: float32 [8, 65536], P('head', 'ctx'), may hold values from 0 to 2
- lengths: int32 [3], replicated, may hold values from 49152 to 65536, as said below
- positions: int32 [3, 64], replicated, may hold values from 49152 to 65599, as said below
Outputs:
- attended: bfloat16 [3, 64, 12288], P(None, 'head', 'ctx')
- eviction: float32 [8, 65536], P('head', 'ctx')
Inputs may be any that keep to these rules, and one draw needn't show every extreme that they name: `lengths`: later steps have more valid tokens; the last step has all 65536. Within a step the positions start at that step's valid length and never fall, rising by at most one from a row to the next; in the last step they rise by exactly one each row.
All inputs are finite; a program needn't handle non-finite values.
Results may differ from a plain program's by a relative error of at most 0.028.
Values may be sent and summed in bfloat16 or wider, within the bound.
A program may use at most 128 MiB of HBM per device.

v0:
```python
import jax
import jax.numpy as jnp
from jax import lax
from jax.sharding import PartitionSpec as P

ROPE_BASE = 1000000.0
NEGATIVE = -1e30


def combined_all(part, axis, combine):
    gathered = jax.tree.map(lambda a: lax.all_gather(a, axis), part)

    def take(source):
        return jax.tree.map(lambda a: lax.dynamic_index_in_dim(a, source, 0, False), gathered)

    return lax.fori_loop(
        1, lax.axis_size(axis), lambda source, state: combine(state, take(source)), take(0)
    )


def rotate(vectors, where_at):
    half = vectors.shape[-1] // 2
    freq = ROPE_BASE ** (-(jnp.arange(half, dtype=jnp.float32) * 2.0 / vectors.shape[-1]))
    angle = where_at.astype(jnp.float32)[:, None] * freq[None, :]
    cosine = jnp.cos(angle)
    sine = jnp.sin(angle)
    first = vectors[..., :half]
    second = vectors[..., half:]
    return jnp.concatenate(
        [first * cosine - second * sine, second * cosine + first * sine], axis=-1
    )


def join_partial(earlier, later):
    top_a, total_a, sums_a = earlier
    top_b, total_b, sums_b = later
    peak = jnp.maximum(top_a, top_b)
    scale_a = jnp.exp(top_a - peak)
    scale_b = jnp.exp(top_b - peak)
    return (
        peak,
        total_a * scale_a + total_b * scale_b,
        sums_a * scale_a[..., None] + sums_b * scale_b[..., None],
    )


def local(
    queries,
    key_latent,
    value_latent,
    key_up,
    value_up,
    out_weight,
    prior_scores,
    lengths,
    positions,
):
    groups, ctx_dev, rank = key_latent.shape
    head_dim = key_up.shape[2]
    q_rows = queries.shape[1]
    all_steps = queries.shape[0]
    pairs = queries.shape[2] // (groups * 2 * head_dim)
    width = out_weight.shape[1]
    key_pos = lax.axis_index("ctx") * ctx_dev + jnp.arange(ctx_dev, dtype=jnp.int32)
    keys = jnp.einsum("gkr,grd->gkd", key_latent, key_up, preferred_element_type=jnp.float32)
    keys = rotate(keys, key_pos).astype(jnp.bfloat16)
    values = jnp.einsum(
        "gkr,grd->gkd", value_latent, value_up, preferred_element_type=jnp.float32
    ).astype(jnp.bfloat16)
    projector = out_weight.reshape(groups, pairs, 2, head_dim, width)
    batches = [(index, 1) for index in range(all_steps)]
    tally = prior_scores
    results = []
    for first_step, group_steps in batches:
        block_q = queries[first_step : first_step + group_steps]
        block_pos = positions[first_step : first_step + group_steps].reshape(group_steps * q_rows)
        block_len = lengths[first_step : first_step + group_steps]
        query_f = (
            block_q.astype(jnp.float32)
            .reshape(group_steps * q_rows, groups * pairs * 2, head_dim)
            .transpose(1, 0, 2)
        )
        query_b = (rotate(query_f, block_pos) * head_dim ** (-0.5)).astype(jnp.bfloat16)
        query_b = query_b.reshape(groups, pairs, 2 * group_steps * q_rows, head_dim).transpose(
            1, 0, 2, 3
        )
        row_step = jnp.arange(2 * group_steps * q_rows, dtype=jnp.int32) // q_rows % group_steps
        live = key_pos[None, :] < block_len[row_step][:, None]

        def block(carry, query_blk):
            scores = jnp.einsum("gnd,gkd->gnk", query_blk, keys, preferred_element_type=jnp.float32)
            scores = jnp.where(live[None], scores, NEGATIVE)
            top = jnp.max(scores, axis=-1)
            expo = jnp.where(live[None], jnp.exp(scores - top[..., None]), 0.0)
            total = jnp.sum(expo, axis=-1)
            weights = expo.astype(jnp.bfloat16)
            sums = jnp.einsum("gnk,gkd->gnd", weights, values, preferred_element_type=jnp.float32)
            return (carry, (top, total, sums, weights))

        unused, (top, total, sums, weights) = lax.scan(block, jnp.zeros((), jnp.float32), query_b)
        top = top.reshape(pairs, groups, 2, group_steps, q_rows)
        total = total.reshape(pairs, groups, 2, group_steps, q_rows)
        sums = sums.reshape(pairs, groups, 2, group_steps, q_rows, head_dim)
        peak, denom, merged = combined_all((top, total, sums), "ctx", join_partial)
        attn = (merged / denom[..., None]).astype(jnp.bfloat16)
        coeff = (
            (jnp.exp(top - peak) / denom)
            .astype(jnp.bfloat16)
            .reshape(pairs, groups, 2 * group_steps * q_rows)
        )
        tally = tally + jnp.einsum(
            "pgn,pgnk->gk", coeff, weights, preferred_element_type=jnp.float32
        )
        product = jnp.einsum(
            "pgasqd,gpade->qse", attn, projector, preferred_element_type=jnp.float32
        )
        owned_rows = lax.psum_scatter(
            product.reshape(
                lax.axis_size("head") * (group_steps * q_rows // lax.axis_size("head")), width
            ).astype(jnp.bfloat16),
            "head",
            scatter_dimension=0,
            tiled=True,
        ).astype(jnp.float32)
        owned_rows = owned_rows.reshape(
            owned_rows.shape[0] // group_steps, group_steps, width
        ).transpose(1, 0, 2)
        results.append(owned_rows.astype(jnp.bfloat16))
    return (jnp.concatenate(results, axis=0), tally)


def solution(mesh):
    placed = (
        P(None, None, "head"),
        P("head", "ctx", None),
        P("head", "ctx", None),
        P("head", None, None),
        P("head", None, None),
        P("head", "ctx"),
        P("head", "ctx"),
        P(),
        P(),
    )
    return jax.shard_map(
        local,
        mesh=mesh,
        in_specs=placed,
        out_specs=(P(None, "head", "ctx"), P("head", "ctx")),
        check_vma=False,
    )
```

profile of v0, /device:TPU:1, one launch (start us, length us, event | category | flops | bytes accessed | tf_op | source)
XLA Modules:
  0.0 570.5 jit_solution(16914511939509320641)
XLA Ops:
  7.2 1.4 fusion.98
  9.5 1.7 convolution_bitcast_fusion.3
  11.2 2.3 fusion.74
  13.8 2.0 slice_convert_fusion.2
  21.0 2.0 broadcast.326.clone.1
  23.1 16.5 %while.112 = (s32[]{:T(128)}, f32[6,1,128]{2,1,0:T(1,128)S(1)}, f32[6,1,128]{2,1,0:T(1,128)S(1)}, f32[6,1,128,128]{3,2,1,0:T(8,128)}, bf16[6,1,128,2048]{3,2,1,0...) while((s32[]{:T(128)}, f32[6,1,128]{2,1,0:T(1,128)S(1)}, ...), condition=%wide.region_10.11_spmd.clone, body=%wide.region_7.10_spmd.clone.sunk | while | flops 137101056 | bytes 5878397 | solution.py:100
  40.1 2.1 broadcast.326.clone
  42.2 12.7 %while.113 = (s32[]{:T(128)}, f32[6,1,128]{2,1,0:T(1,128)S(1)}, f32[6,1,128]{2,1,0:T(1,128)S(1)}, f32[6,1,128,128]{3,2,1,0:T(8,128)S(1)}, bf16[6,1,128,2048]{3,2...) while((s32[]{:T(128)}, f32[6,1,128]{2,1,0:T(1,128)S(1)}, ...), condition=%wide.region_17.18_spmd.clone, body=%wide.region_14.17_spmd.clone.sunk | while | flops 137101056 | bytes 5878397 | solution.py:100
  58.0 2.1 broadcast.326.clone.2
  60.1 12.8 %while.111 = (s32[]{:T(128)}, f32[6,1,128]{2,1,0:T(1,128)S(1)}, f32[6,1,128]{2,1,0:T(1,128)S(1)}, f32[6,1,128,128]{3,2,1,0:T(8,128)S(1)}, bf16[6,1,128,2048]{3,2...) while((s32[]{:T(128)}, f32[6,1,128]{2,1,0:T(1,128)S(1)}, ...), condition=%wide.region_3.4_spmd.clone, body=%wide.region_0.3_spmd.clone.sunk | while | flops 137101056 | bytes 5878397 | solution.py:100
  74.3 42.8 %all_gather.30 = f32[32,6,1,2,1,64]{5,3,4,2,1,0:T(2,128)S(1)} all-gather(f32[1,6,1,2,1,64]{5,3,4,2,1,0:T(2,128)S(1)} %all_gather_reshape.30), channel_id=1, replica_groups=mesh['ctx'=32,'head'=8] {'ctx'}, dimensions={0}, use_global_device_ids=true | all-gather | bytes 101376 | tf_op jit(solution)/shard_map/all_gather | solution.py:11
  117.1 38.5 %all_gather.31 = f32[32,6,1,2,1,64]{5,3,4,2,1,0:T(2,128)S(1)} all-gather(f32[1,6,1,2,1,64]{5,3,4,2,1,0:T(2,128)S(1)} %all_gather_reshape.31), channel_id=1, replica_groups=mesh['ctx'=32,'head'=8] {'ctx'}, dimensions={0}, use_global_device_ids=true | all-gather | bytes 101376 | tf_op jit(solution)/shard_map/all_gather | solution.py:11
  155.7 35.8 %all_gather.33 = f32[32,6,1,2,1,64]{5,3,4,2,1,0:T(2,128)S(1)} all-gather(f32[1,6,1,2,1,64]{5,3,4,2,1,0:T(2,128)S(1)} %all_gather_reshape.33), channel_id=1, replica_groups=mesh['ctx'=32,'head'=8] {'ctx'}, dimensions={0}, use_global_device_ids=true | all-gather | bytes 101376 | tf_op jit(solution)/shard_map/all_gather | solution.py:11
  191.5 37.4 %all_gather.34 = f32[32,6,1,2,1,64]{5,3,4,2,1,0:T(2,128)S(1)} all-gather(f32[1,6,1,2,1,64]{5,3,4,2,1,0:T(2,128)S(1)} %all_gather_reshape.34), channel_id=1, replica_groups=mesh['ctx'=32,'head'=8] {'ctx'}, dimensions={0}, use_global_device_ids=true | all-gather | bytes 101376 | tf_op jit(solution)/shard_map/all_gather | solution.py:11
  229.0 38.8 %all_gather.27 = f32[32,6,1,2,1,64]{5,3,4,2,1,0:T(2,128)S(1)} all-gather(f32[1,6,1,2,1,64]{5,3,4,2,1,0:T(2,128)S(1)} %all_gather_reshape.27), channel_id=1, replica_groups=mesh['ctx'=32,'head'=8] {'ctx'}, dimensions={0}, use_global_device_ids=true | all-gather | bytes 101376 | tf_op jit(solution)/shard_map/all_gather | solution.py:11
  267.7 36.3 %all_gather.28 = f32[32,6,1,2,1,64]{5,3,4,2,1,0:T(2,128)S(1)} all-gather(f32[1,6,1,2,1,64]{5,3,4,2,1,0:T(2,128)S(1)} %all_gather_reshape.28), channel_id=1, replica_groups=mesh['ctx'=32,'head'=8] {'ctx'}, dimensions={0}, use_global_device_ids=true | all-gather | bytes 101376 | tf_op jit(solution)/shard_map/all_gather | solution.py:11
  306.3 45.3 %while.109 = (s32[]{:T(128)}, f32[6,1,2,1,64]{4,3,2,1,0:T(1,128)S(1)}, f32[6,1,2,1,64]{4,3,2,1,0:T(1,128)S(1)}, f32[6,1,2,1,64,128]{5,4,3,2,1,0:T(8,128)S(1)}, f...) while((s32[]{:T(128)}, ...), condition=%wide.region_12.13_spmd, body=%wide.region_11.12_spmd.sunk | while | flops 299525 | bytes 1222799 | solution.py:16
  306.4 1.4 fusion.127
  307.9 1.4 fusion.127
  309.3 1.4 fusion.127
  310.8 1.4 fusion.127
  312.2 1.4 fusion.127
  313.7 1.4 fusion.127
  315.2 1.4 fusion.127
  316.6 1.4 fusion.127
  318.1 1.4 fusion.127
  319.5 1.4 fusion.127
  321.0 1.4 fusion.127
  322.5 1.4 fusion.127
  323.9 1.4 fusion.127
  325.4 1.4 fusion.127
  326.8 1.4 fusion.127
  334.1 1.4 fusion.127
  337.0 1.4 fusion.127
  338.5 1.4 fusion.127
  344.4 1.4 fusion.127
  345.8 1.4 fusion.127
  347.3 1.4 fusion.127
  350.2 1.4 fusion.127
  352.8 45.4 %while.110 = (s32[]{:T(128)}, f32[6,1,2,1,64]{4,3,2,1,0:T(1,128)S(1)}, f32[6,1,2,1,64]{4,3,2,1,0:T(1,128)S(1)}, f32[6,1,2,1,64,128]{5,4,3,2,1,0:T(8,128)S(1)}, f...) while((s32[]{:T(128)}, ...), condition=%wide.region_19.20_spmd, body=%wide.region_18.19_spmd.sunk | while | flops 299525 | bytes 1222799 | solution.py:16
  354.3 1.4 fusion.128
  355.8 1.4 fusion.128
  358.7 1.4 fusion.128
  360.2 1.4 fusion.128
  361.7 1.4 fusion.128
  364.6 1.4 fusion.128
  366.1 1.4 fusion.128
  367.6 1.4 fusion.128
  369.0 1.4 fusion.128
  371.9 1.4 fusion.128
  373.4 1.4 fusion.128
  376.3 1.4 fusion.128
  379.2 1.4 fusion.128
  383.6 1.4 fusion.128
  385.1 1.4 fusion.128
  388.0 1.4 fusion.128
  392.4 1.4 fusion.128
  393.9 1.4 fusion.128
  398.3 6.5 %all-gather.4.cloned.1.call-done = f32[32,6,1,2,1,64,128]{6,5,4,3,2,1,0:T(8,128)} async-done(((f32[1,6,1,2,1,64,128]{6,5,4,3,2,1,0:T(8,128)}), f32[32,6,1,2,1,64,128]{6,5,4,3,2,1,0:T(8,128)}) %all-gather.4.cloned.1.call-update) | async-done | bytes 12582928 | tf_op jit(solution)/shard_map/all_gather | solution.py:11
  405.8 45.2 %while.108 = (s32[]{:T(128)}, f32[6,1,2,1,64]{4,3,2,1,0:T(1,128)S(1)}, f32[6,1,2,1,64]{4,3,2,1,0:T(1,128)S(1)}, f32[6,1,2,1,64,128]{5,4,3,2,1,0:T(8,128)S(1)}, f...) while((s32[]{:T(128)}, ...), condition=%wide.region_5.6_spmd, body=%wide.region_4.5_spmd.sunk | while | flops 299525 | bytes 1222799 | solution.py:16
  426.3 1.4 fusion.126
  454.1 2.6 fusion.58
  457.4 3.0 fusion.52
  460.5 100.8 %all-reduce.6.cloned.1.call-done = (bf16[64,384]{1,0:T(8,128)(2,1)}, bf16[64,384]{1,0:T(8,128)(2,1)}, bf16[64,384]{1,0:T(8,128)(2,1)}) async-done(((bf16[64,384]{1,0:T(8,128)(2,1)}, bf16[64,384]{1,0:T(8,128)(2,1)}, bf16[64,384]{1,0:T(8,128)(2,1)}), (bf16[64,384]{1,0:T(8,128)(2,1)}, bf16[64,384]{1,0:T(8,128)(2,1)}, bf16[64,384]{1,0:T(8,128)(2,1)})) %all-reduce.6.cloned.1.call-update) | async-done | bytes 147472
  (433 shorter events, 139.8 us)
Async XLA Ops:
  7.2 443.9 %copy-start = (bf16[1536,384]{1,0:T(8,128)(2,1)S(1)}, bf16[1536,384]{1,0:T(8,128)(2,1)}, u32[]{:S(2)}) copy-start(bf16[1536,384]{1,0:T(8,128)(2,1)} %param.26) | copy-start | bytes 3538948
  7.2 298.1 %all-gather.6.cloned.1.call-start = ((), (), s32[]{:S(2)}) async-start(), calls=%async_computation.1 | async-start | bytes 12976128 | tf_op jit(solution)/shard_map/all_gather | solution.py:11
  16.0 3.7 copy-start.6
  16.0 3.7 copy-start.7
  23.1 16.5 %copy-start.2 = (f32[12,64,64]{2,0,1:T(8,128)S(1)}, f32[12,64,64]{2,0,1:T(8,128)}, u32[]{:S(2)}) copy-start(f32[12,64,64]{2,0,1:T(8,128)} %get-tuple-element.1037) | copy-start | bytes 589828
  39.6 312.2 %all-gather.8.cloned.1.call-start = ((), (), s32[]{:S(2)}) async-start(), calls=%async_computation.2 | async-start | bytes 12976128 | tf_op jit(solution)/shard_map/all_gather | solution.py:11
  42.2 13.5 %copy-start.3 = (f32[1,64,1536]{2,1,0:T(8,128)S(1)}, f32[1,64,1536]{2,1,0:T(8,128)}, u32[]{:S(2)}) copy-start(f32[1,64,1536]{2,1,0:T(8,128)} %get-tuple-element.1032) | copy-start | bytes 1179652
  54.9 0.8 copy-start.5
  54.9 0.8 copy-start.8
  55.7 349.1 %all-gather.4.cloned.1.call-start = ((), (), s32[]{:S(2)}) async-start(), calls=%async_computation | async-start | bytes 12976128 | tf_op jit(solution)/shard_map/all_gather | solution.py:11
  60.1 13.8 %copy-start.9 = (f32[6,1,128]{2,1,0:T(1,128)S(1)}, f32[6,1,128]{2,1,0:T(1,128)}, u32[]{:S(2)}) copy-start(f32[6,1,128]{2,1,0:T(1,128)} %copy-done.8) | copy-start | bytes 9220
  60.1 243.9 %copy-start.11 = (u32[256]{0:T(256)S(1)}, u32[256]{0:T(256)}, u32[]{:S(2)}) copy-start(u32[256]{0:T(256)} %constant.254) | copy-start | bytes 3076
  72.9 0.8 copy-start.4
  73.7 487.6 %all-reduce.6.cloned.1.call-start = ((), (), s32[]{:S(2)}) async-start(), calls=%async_computation.3 | async-start | bytes 294912
  452.1 2.0 copy-start.10
  454.1 2.8 copy-start.1
Sparse Core Ops, SparseCore 0:
  39.7 125.4 all-gather.5
  167.7 117.9 all-gather.7
  288.3 116.4 all-gather.3
  457.6 103.6 all-reduce.5
where the time goes:
time: 576 us; the launch traced here: 570 us
  blocking collectives  229 us (40%)
  other arithmetic  168 us (29%)
  waiting for transfers between devices  107 us (19%)
  matrix products  28.2 us (5%)
  local copies, waits for them, and re-layouts  19.3 us (3%)
  between operations  14.8 us (3%)
    all_gather x6, blocking collectives, combined_all(): gathered = jax.tree.map(lambda a: lax.all_gather(a, axis), part)  229 us
    add x93, other arithmetic, join_partial(): sums_a * scale_a[..., None] + sums_b * scale_b[..., None]  129 us
    unnamed x5, waiting for transfers between devices  101 us
    dynamic_update_slice x18, other arithmetic, local(): lax.scan(block, jnp.zeros((), jnp.float32), query_b)  18.6 us
  transfers between devices with their start and end apart: 4, of which 2 were waited for; matrix products, arithmetic and copies ran while one was open for 22% of the time, Pallas kernels for 0%

commit v1 on v0

v1 whole, which is shorter than its diff:
```python
import functools

import jax
import jax.numpy as jnp
import numpy as np
from jax import lax
from jax.experimental import pallas as pl
from jax.experimental.pallas import tpu as pltpu
from jax.sharding import PartitionSpec as P

ROPE_BASE = 1000000.0
NEGATIVE = -1e30
BF16 = jnp.bfloat16
F32 = jnp.float32
MESH = pl.DeviceIdType.MESH

NX, NZ, NHEAD = 4, 8, 8
STEPS, ROWS = 3, 64
HEADS, DIM, RANK = 12, 128, 256
TOKENS = 2048
WIDTH = 384
LIVE = STEPS * (ROWS // NZ)
BLOCK = LIVE + 8
PAD = NZ * BLOCK
HROWS = STEPS * ROWS
PAIR = 2
GROUP = NX
GROUPS = HEADS // GROUP
UNITS = HEADS // PAIR
LANES = 128


def rotary_tables():
    half = DIM // 2
    freq = (ROPE_BASE ** (-(np.arange(half) * 2.0 / DIM))).astype(np.float32).astype(np.float64)
    starts = np.arange(NX * NZ * TOKENS // LANES, dtype=np.float64) * LANES
    coarse = freq[:, None] * starts[None, :]
    coarse = coarse.reshape(half, -1, LANES).transpose(1, 0, 2)
    fine = freq[:, None] * np.arange(LANES, dtype=np.float64)[None, :]
    pair = lambda a, axis: np.stack([np.cos(a), np.sin(a)], axis=axis).astype(np.float32)
    row = np.concatenate([freq, freq]).astype(np.float32)[None, :]
    return pair(coarse, 1), pair(fine, 0), np.broadcast_to(row, (8, DIM)).copy()


def three(x):
    hi = x.astype(BF16).astype(F32)
    rest = x - hi
    mid = rest.astype(BF16).astype(F32)
    return hi, mid, rest - mid


def two(x):
    hi = x.astype(BF16).astype(F32)
    return hi, x - hi


def stack_rows(rows):
    sub = lax.broadcasted_iota(jnp.int32, (8, LANES), 0)
    out = jnp.zeros((8, LANES), F32)
    for index, row in enumerate(rows):
        out = jnp.where(sub == index, row, out)
    return out


def top_of(stats):
    return stats[0:1] + stats[1:2] + stats[2:3]


def total_of(stats):
    return stats[3:4] + stats[4:5]


def join(stats):
    tops = [top_of(s) for s in stats]
    peak = functools.reduce(jnp.maximum, tops)
    factors = [jnp.exp(t - peak) for t in tops]
    total = functools.reduce(jnp.add, [f * total_of(s) for f, s in zip(factors, stats)])
    return peak, total, factors


def kernel(
    q_hbm, kl_hbm, vl_hbm, ku_ref, vu_ref, w_hbm, prior_ref, len_ref, pos_ref, coarse_ref, fine_ref, freq_ref,
    out_ref, ev_ref,
    q_v, kl_v, vl_v, w_v, qa, keys, values, pos_v, score_a, score_b, weights, stat_v,
    xw, xr, zw, zr, ft, ax, acc, hw, hr,
    load_sem, xs_sem, xr_sem, zs_sem, zr_sem, as_sem, ar_sem, bs_sem, br_sem, hs_sem, hr_sem,
):
    ctx = lax.axis_index("ctx")
    head = lax.axis_index("head")
    z = ctx // NX
    x = lax.rem(ctx, NX)

    loads = [
        pltpu.make_async_copy(src, dst, load_sem.at[i])
        for i, (src, dst) in enumerate([(kl_hbm.at[0], kl_v), (q_hbm, q_v), (vl_hbm.at[0], vl_v), (w_hbm, w_v)])
    ]
    for load in loads:
        load.start()

    def at_x(d):
        return {"ctx": z * NX + lax.rem(x + d, NX), "head": head}

    def at_z(d):
        return {"ctx": lax.rem(z + d, NZ) * NX + x, "head": head}

    def at_head(d):
        return {"ctx": ctx, "head": lax.rem(head + d, NHEAD)}

    peers = [at_x(d) for d in range(1, NX)] + [at_z(d) for d in range(1, NZ)] + [at_head(d) for d in range(1, NHEAD)]
    barrier = pltpu.get_barrier_semaphore()
    for peer in peers:
        pl.semaphore_signal(barrier, inc=1, device_id=peer, device_id_type=MESH)

    def send(src, dst, s_sem, r_sem, peer):
        copy = pltpu.make_async_remote_copy(
            src_ref=src, dst_ref=dst, send_sem=s_sem, recv_sem=r_sem, device_id=peer, device_id_type=MESH
        )
        copy.start()
        return copy

    pos_v[...] = jnp.zeros_like(pos_v)
    pos_v[0:STEPS, 0:ROWS] = pos_ref[...].astype(F32)
    pos_t = jnp.transpose(pos_v[...])
    where_at = jnp.concatenate(
        [pos_t[8 * p : 8 * p + 8, s : s + 1] for p in range(NZ) for s in range(STEPS)], axis=0
    )
    angle = where_at * freq_ref[0:1, :]
    lane = lax.broadcasted_iota(jnp.int32, (HROWS, DIM), 1)
    cos_q = jnp.cos(angle)
    sin_q = jnp.where(lane < DIM // 2, -jnp.sin(angle), jnp.sin(angle))
    row_step = jnp.concatenate(
        [jnp.full((8, DIM), s, jnp.int32) for p in range(NZ) for s in range(STEPS)], axis=0
    )
    marks = jnp.where(lane == row_step, 1.0, 0.0).astype(BF16)

    loads[0].wait()
    key_up = jnp.transpose(ku_ref[0].astype(F32)).astype(BF16)
    coarse = coarse_ref[lax.div(ctx, 8)]
    shift = lax.rem(LANES - lax.rem(ctx, 8) * (TOKENS // LANES), LANES)
    cos_c = pltpu.roll(coarse[0], shift, 1)
    sin_c = pltpu.roll(coarse[1], shift, 1)
    cos_f = fine_ref[0]
    sin_f = fine_ref[1]
    half = DIM // 2
    chunk = 512
    for start in range(0, TOKENS, chunk):
        raw = lax.dot_general(
            key_up, kl_v[start : start + chunk, :], (((1,), (1,)), ((), ())), preferred_element_type=F32
        )
        for off in range(0, chunk, LANES):
            a = (start + off) // LANES
            ca, sa = cos_c[:, a : a + 1], sin_c[:, a : a + 1]
            cosine = ca * cos_f - sa * sin_f
            sine = sa * cos_f + ca * sin_f
            first, second = raw[:half, off : off + LANES], raw[half:, off : off + LANES]
            keys[0:half, start + off : start + off + LANES] = (first * cosine - second * sine).astype(BF16)
            keys[half:DIM, start + off : start + off + LANES] = (second * cosine + first * sine).astype(BF16)
    token = ctx * TOKENS + lax.broadcasted_iota(jnp.int32, (16, TOKENS), 1)
    step_row = lax.broadcasted_iota(jnp.int32, (16, TOKENS), 0)
    limit = jnp.where(step_row == 0, len_ref[0], jnp.where(step_row == 1, len_ref[1], len_ref[2]))
    dead = (step_row < STEPS) & (token >= limit)
    keys[DIM : DIM + 16, :] = jnp.where(dead, NEGATIVE, 0.0).astype(BF16)
    keys[DIM + 16 : 2 * DIM, :] = jnp.zeros((DIM - 16, TOKENS), BF16)

    loads[1].wait()
    for h in range(HEADS):
        block = [q_v[s, :, h * DIM : (h + 1) * DIM].astype(F32) for s in range(STEPS)]
        rows = jnp.concatenate([block[s][8 * p : 8 * p + 8] for p in range(NZ) for s in range(STEPS)], axis=0)
        turned = (rows * cos_q + pltpu.roll(rows, half, 1) * sin_q) * (DIM**-0.5)
        qa[h * HROWS : (h + 1) * HROWS, 0:DIM] = turned.astype(BF16)
        qa[h * HROWS : (h + 1) * HROWS, DIM : 2 * DIM] = marks

    loads[2].wait()
    values[...] = jnp.dot(vl_v[...], vu_ref[0], preferred_element_type=F32).astype(BF16)

    span = PAIR * HROWS

    def scores(u, dst):
        dst[...] = jnp.dot(qa[u * span : (u + 1) * span, :], keys[...], preferred_element_type=F32)

    stat_lane = lax.broadcasted_iota(jnp.int32, (HROWS, LANES), 1)
    filler = jnp.where(lax.broadcasted_iota(jnp.int32, (8, LANES), 1) == 3, 1.0, 0.0)

    def soft(u, src):
        s = src[...]
        top = jnp.max(s, axis=1, keepdims=True)
        expo = jnp.exp(s - top)
        total = jnp.sum(expo, axis=1, keepdims=True)
        w = expo.astype(BF16)
        weights[u * span : (u + 1) * span, :] = w
        sums = jnp.dot(w, values[...], preferred_element_type=F32)
        for i in range(PAIR):
            h = u * PAIR + i
            rows = slice(i * HROWS, (i + 1) * HROWS)
            columns = jnp.zeros((HROWS, LANES), F32)
            for k, part in enumerate((*three(top[rows]), *two(total[rows]))):
                columns = jnp.where(stat_lane == k, part, columns)
            spread = []
            for p in range(NZ):
                spread += [columns[LIVE * p : LIVE * (p + 1)], filler]
            stats = jnp.transpose(jnp.concatenate(spread, axis=0))[0:8]
            stat_v[h] = stats
            for p in range(NZ):
                half_stats = stats[:, LANES * (p // 4) : LANES * (p // 4 + 1)]
                piece = jnp.concatenate([sums[rows][LIVE * p : LIVE * (p + 1)], half_stats], axis=0)
                xw[h, BLOCK * p : BLOCK * (p + 1), :] = piece.astype(BF16)

    sent = []

    def send_x(g):
        for d in range(1, NX):
            there = g * GROUP + lax.rem(x + d, NX)
            sent.append(send(xw.at[there], xr.at[g, d - 1], xs_sem.at[g, d - 1], xr_sem.at[g, d - 1], at_x(d)))

    def wait_for(dst, sem):
        pltpu.make_async_copy(dst, dst, sem).wait()

    def merge_x(g):
        for d in range(1, NX):
            wait_for(xr.at[g, d - 1], xr_sem.at[g, d - 1])
        mine = g * GROUP + x

        def piece(c, p):
            ref = xw.at[mine] if c == 0 else xr.at[g, c - 1]
            return ref[BLOCK * p : BLOCK * (p + 1), :].astype(F32)

        for q in range(NZ // 4):
            first = [piece(c, 4 * q) for c in range(NX)]
            peak, total, factors = join([f[LIVE:] for f in first])
            by_row = jnp.transpose(stack_rows(factors))
            stats = stack_rows((*three(peak), *two(total)))
            for b in range(4):
                p = 4 * q + b
                merged = functools.reduce(
                    jnp.add,
                    [
                        (first[c] if b == 0 else piece(c, p))[:LIVE] * by_row[BLOCK * b : BLOCK * b + LIVE, c : c + 1]
                        for c in range(NX)
                    ],
                )
                zw[g, BLOCK * p : BLOCK * (p + 1), :] = jnp.concatenate([merged, stats], axis=0).astype(BF16)

    def send_z(g):
        for d in range(1, NZ):
            there = lax.rem(z + d, NZ)
            src = zw.at[g, pl.ds(pl.multiple_of(there * BLOCK, BLOCK), BLOCK)]
            sent.append(send(src, zr.at[g, d - 1], zs_sem.at[g, d - 1], zr_sem.at[g, d - 1], at_z(d)))

    def mine_z():
        return pl.ds(pl.multiple_of(z * BLOCK, BLOCK), BLOCK)

    def merge_z(g):
        for d in range(1, NZ):
            wait_for(zr.at[g, d - 1], zr_sem.at[g, d - 1])
        pieces = [zw[g, mine_z(), :].astype(F32)] + [zr[g, i].astype(F32) for i in range(NZ - 1)]
        peak, total, factors = join([p[LIVE:] for p in pieces])
        scale = 1.0 / total
        ft[:, 0:8] = jnp.transpose(stack_rows([f * scale for f in factors]))
        by_row = ft[pl.ds(pl.multiple_of(lax.rem(z, 4) * BLOCK, BLOCK), LIVE), 0:8]
        merged = functools.reduce(jnp.add, [p[:LIVE] * by_row[:, c : c + 1] for c, p in enumerate(pieces)])
        stats = stack_rows((*three(peak), *two(total)))
        ax[g * GROUP + x, mine_z(), :] = jnp.concatenate([merged, stats], axis=0).astype(BF16)

    def share_z(g):
        here = ax.at[g * GROUP + x, mine_z()]
        for d in range(1, NZ):
            sent.append(send(here, here, as_sem.at[g, d - 1], ar_sem.at[g, d - 1], at_z(d)))

    def share_x(g):
        for d in range(1, NZ):
            here = ax.at[g * GROUP + x, mine_z()]
            wait_for(here, ar_sem.at[g, d - 1])
        here = ax.at[g * GROUP + x]
        for d in range(1, NX):
            sent.append(send(here, here, bs_sem.at[g, d - 1], br_sem.at[g, d - 1], at_x(d)))

    def gathered(g):
        for d in range(1, NX):
            here = ax.at[g * GROUP + x]
            wait_for(here, br_sem.at[g, d - 1])

    def project(g):
        rows = jnp.concatenate([ax[g * GROUP + i] for i in range(GROUP)], axis=1)
        part = jnp.dot(rows, w_v[g * GROUP * DIM : (g + 1) * GROUP * DIM, :], preferred_element_type=F32)
        acc[...] = part if g == 0 else acc[...] + part

    pick_r = lax.broadcasted_iota(jnp.int32, (PAD, HROWS), 0)
    pick_c = lax.broadcasted_iota(jnp.int32, (PAD, HROWS), 1)
    low = pick_r & (BLOCK - 1)
    pick = jnp.where((low < LIVE) & (pick_r - 8 * (pick_r >> 5) == pick_c), 1.0, 0.0).astype(BF16)
    slot = lax.broadcasted_iota(jnp.int32, (8, LANES), 1)

    def evict(g):
        tally = jnp.zeros((16, TOKENS), F32)
        for i in range(GROUP):
            h = g * GROUP + i
            sides = []
            for q in range(NZ // 4):
                stats = jnp.zeros((8, LANES), F32)
                for b in range(4):
                    p = 4 * q + b
                    whole = ax[h, BLOCK * p : BLOCK * (p + 1), :].astype(F32)
                    stats = jnp.where(slot >> 5 == b, whole[LIVE:], stats)
                own = top_of(stat_v[h][:, q * LANES : (q + 1) * LANES])
                coeff = jnp.exp(own - top_of(stats)) / total_of(stats)
                sides.append(jnp.where((slot[0:1] & (BLOCK - 1)) < LIVE, coeff, 0.0))
            coeff = jnp.broadcast_to(jnp.concatenate(sides, axis=1), (16, PAD)).astype(BF16)
            coeff = jnp.dot(coeff, pick, preferred_element_type=F32).astype(BF16)
            tally = tally + jnp.dot(coeff, weights[h * HROWS : (h + 1) * HROWS, :], preferred_element_type=F32)
        if g == 0:
            ev_ref[...] = prior_ref[...] + tally[0:1]
        else:
            ev_ref[...] = ev_ref[...] + tally[0:1]

    scores(0, score_a)
    for u in range(UNITS):
        now, later = (score_a, score_b) if u % 2 == 0 else (score_b, score_a)
        if u + 1 < UNITS:
            scores(u + 1, later)
        soft(u, now)
        if u == 1:
            pl.semaphore_wait(barrier, len(peers))
        if u % 2 == 1:
            send_x(u // 2)
    for g in range(GROUPS):
        merge_x(g)
        send_z(g)
    for g in range(GROUPS):
        merge_z(g)
        share_z(g)
    for g in range(GROUPS):
        share_x(g)
    loads[3].wait()
    for g in range(GROUPS):
        gathered(g)
        project(g)
        if g + 1 < GROUPS:
            evict(g)
    hw[...] = acc[...].astype(BF16)
    for d in range(1, NHEAD):
        there = lax.rem(head + d, NHEAD)
        src = hw.at[pl.ds(pl.multiple_of(there * BLOCK, BLOCK), BLOCK)]
        sent.append(send(src, hr.at[d - 1], hs_sem.at[d - 1], hr_sem.at[d - 1], at_head(d)))
    evict(GROUPS - 1)
    final = acc[pl.ds(pl.multiple_of(head * BLOCK, BLOCK), BLOCK), :]
    for d in range(1, NHEAD):
        wait_for(hr.at[d - 1], hr_sem.at[d - 1])
        final = final + hr[d - 1].astype(F32)
    for s in range(STEPS):
        out_ref[s] = final[8 * s : 8 * s + 8].astype(BF16)
    for copy in sent:
        copy.wait_send()


def local(queries, key_latent, value_latent, key_up, value_up, out_weight, prior, lengths, positions):
    coarse, fine, freq = rotary_tables()
    vmem = pl.BlockSpec(memory_space=pltpu.VMEM)
    smem = pl.BlockSpec(memory_space=pltpu.SMEM)
    hbm = pl.BlockSpec(memory_space=pl.ANY)
    dma = pltpu.SemaphoreType.DMA
    return pl.pallas_call(
        kernel,
        out_shape=(
            jax.ShapeDtypeStruct((STEPS, ROWS // NHEAD, WIDTH), BF16),
            jax.ShapeDtypeStruct((1, TOKENS), F32),
        ),
        in_specs=[hbm, hbm, hbm, vmem, vmem, hbm, vmem, smem, vmem, vmem, vmem, vmem],
        out_specs=(vmem, vmem),
        scratch_shapes=[
            pltpu.VMEM((STEPS, ROWS, HEADS * DIM), BF16),
            pltpu.VMEM((TOKENS, RANK), BF16),
            pltpu.VMEM((TOKENS, RANK), BF16),
            pltpu.VMEM((HEADS * DIM, WIDTH), BF16),
            pltpu.VMEM((HEADS * HROWS, 2 * DIM), BF16),
            pltpu.VMEM((2 * DIM, TOKENS), BF16),
            pltpu.VMEM((TOKENS, DIM), BF16),
            pltpu.VMEM((8, LANES), F32),
            pltpu.VMEM((PAIR * HROWS, TOKENS), F32),
            pltpu.VMEM((PAIR * HROWS, TOKENS), F32),
            pltpu.VMEM((HEADS * HROWS, TOKENS), BF16),
            pltpu.VMEM((HEADS, 8, PAD), F32),
            pltpu.VMEM((HEADS, PAD, DIM), BF16),
            pltpu.VMEM((GROUPS, NX - 1, PAD, DIM), BF16),
            pltpu.VMEM((GROUPS, PAD, DIM), BF16),
            pltpu.VMEM((GROUPS, NZ - 1, BLOCK, DIM), BF16),
            pltpu.VMEM((LANES, LANES), F32),
            pltpu.VMEM((HEADS, PAD, DIM), BF16),
            pltpu.VMEM((PAD, WIDTH), F32),
            pltpu.VMEM((PAD, WIDTH), BF16),
            pltpu.VMEM((NHEAD - 1, BLOCK, WIDTH), BF16),
            dma((4,)),
            dma((GROUPS, NX - 1)),
            dma((GROUPS, NX - 1)),
            dma((GROUPS, NZ - 1)),
            dma((GROUPS, NZ - 1)),
            dma((GROUPS, NZ - 1)),
            dma((GROUPS, NZ - 1)),
            dma((GROUPS, NX - 1)),
            dma((GROUPS, NX - 1)),
            dma((NHEAD - 1,)),
            dma((NHEAD - 1,)),
        ],
        compiler_params=pltpu.CompilerParams(
            collective_id=0, has_side_effects=True, vmem_limit_bytes=56 * 2**20
        ),
        cost_estimate=pl.CostEstimate(flops=3_500_000_000, bytes_accessed=5_000_000, transcendentals=5_000_000),
        name="decode_attention",
    )(
        queries, key_latent, value_latent, key_up, value_up, out_weight, prior, lengths, positions,
        jnp.asarray(coarse), jnp.asarray(fine), jnp.asarray(freq),
    )


def solution(mesh):
    placed = (
        P(None, None, "head"),
        P("head", "ctx", None),
        P("head", "ctx", None),
        P("head", None, None),
        P("head", None, None),
        P("head", "ctx"),
        P("head", "ctx"),
        P(),
        P(),
    )
    return jax.shard_map(
        local,
        mesh=mesh,
        in_specs=placed,
        out_specs=(P(None, "head", "ctx"), P("head", "ctx")),
        check_vma=False,
    )
```

time: 576 us -> 51.2 us (0.09)
  blocking collectives: 229 us -> 0 us
  other arithmetic: 168 us -> 0 us
  waiting for transfers between devices: 107 us -> 0 us
  Pallas kernels: 0 us -> 47.7 us
  matrix products: 28.2 us -> 0 us
  local copies, waits for them, and re-layouts: 19.3 us -> 2.63 us
  between operations: 14.8 us -> 0.64 us
    all_gather x6 -> x0, blocking collectives: 229 us -> none  [combined_all(): gathered = jax.tree.map(lambda a: lax.all_gather(a, axis), part)]
    add x186 -> x0, other arithmetic: 132 us -> none  [the longest x93 129 us: join_partial(): sums_a * scale_a[..., None] + sums_b * scale_b[..., None]]
    unnamed x5 -> x0, waiting for transfers between devices: 101 us -> none
    pallas_call x0 -> x1, Pallas kernels: none -> 47.7 us  [local(): pl.pallas_call(kernel, out_shape=(jax.ShapeDtypeStruct((STEPS, ROWS // NH...]
    dot_general x44 -> x0, matrix products: 28.2 us -> none  [the longest x18 10.3 us: block(): jnp.einsum('gnk,gkd->gnd', weights, values, preferred_element_type=jnp.fl...]
    dynamic_update_slice x18 -> x0, other arithmetic: 18.6 us -> none  [local(): lax.scan(block, jnp.zeros((), jnp.float32), query_b)]
    another operation x21 -> x0, local copies, waits for them, and re-layouts: 7.76 us -> none
    all_gather x3 -> x0, waiting for transfers between devices: 6.5 us -> none  [combined_all(): gathered = jax.tree.map(lambda a: lax.all_gather(a, axis), part)]
  transfers between devices with their start and end apart: 4 -> 0, of which waited for: 2 -> 0; matrix products, arithmetic and copies ran while one was open for 22% -> 0% of each run, Pallas kernels for 0% -> 0%
where the time goes in v1:
time: 51.2 us; the launch traced here: 51 us
  Pallas kernels  47.7 us (93%)
  local copies, waits for them, and re-layouts  2.63 us (5%)
  between operations  0.64 us (1%)
    pallas_call x1, Pallas kernels, local(): pl.pallas_call(kernel, out_shape=(jax.ShapeDtypeStruct((STEPS, ROWS // NH...  47.7 us
    unnamed x2, local copies, waits for them, and re-layouts  2.63 us

profile of v1, /device:TPU:1, one launch (start us, length us, event | category | flops | bytes accessed | tf_op | source)
XLA Modules:
  0.0 51.0 jit_solution(6569034279291291583)
XLA Ops:
  0.6 47.7 %decode_attention.1 = (bf16[3,8,384]{2,1,0:T(8,128)(2,1)}, f32[1,2048]{1,0:T(1,128)}) custom-call(bf16[3,64,1536]{2,1,0:T(8,128)(2,1)} %q_hbm.1, bf16[1,2048,256]{2,1,0:T(8,128)(2,1)} %kl_hbm.1, bf16[1,2048,256]{2,1,0:T(8,128)(2,1)} %vl_hbm.1, bf16[1,256,128]{2,1,0:T(8,128)(2,1)} %ku_ref.1, bf16[1,256,128]{2,1,0:T(8,128)(2,1)} %vu_ref.1, ...), custom_call_target="tpu_custom_call" | custom-call | flops 3500000000 | bytes 5000000 | tf_op jit(solution)/shard_map/decode_attention/pallas_call | solution.py:361
  48.4 1.3 %copy.16 = bf16[3,8,384]{2,1,0:T(8,128)(2,1)} copy(bf16[3,8,384]{2,1,0:T(8,128)(2,1)} %get-tuple-element.4) | data formatting | bytes 36864
  49.7 1.3 %copy.17 = f32[1,2048]{1,0:T(1,128)} copy(f32[1,2048]{1,0:T(1,128)} %get-tuple-element.5) | data formatting | bytes 16384

commit v2 on v1

v2 whole, which is shorter than its diff:
```python
import functools

import jax
import jax.numpy as jnp
import numpy as np
from jax import lax
from jax.experimental import pallas as pl
from jax.experimental.pallas import tpu as pltpu
from jax.sharding import PartitionSpec as P

ROPE_BASE = 1000000.0
NEGATIVE = -1e30
BF16 = jnp.bfloat16
F32 = jnp.float32
MESH = pl.DeviceIdType.MESH

NX, NZ, NHEAD = 4, 8, 8
STEPS, ROWS = 3, 64
HEADS, DIM, RANK = 12, 128, 256
TOKENS = 2048
WIDTH = 384
LIVE = STEPS * (ROWS // NZ)
BLOCK = LIVE + 8
PAD = NZ * BLOCK
HROWS = STEPS * ROWS
MOST = 3
GROUP = NX
GROUPS = HEADS // GROUP
UNITS = ((0, 2), (2, 2), (4, 2), (6, 2), (8, 1), (9, 1), (10, 1), (11, 1))
WIRE = HROWS + 16
FAR_X = (2, 1, 3)
AWAY = GROUPS * (NX - 1)
FAR_Z = (4, 3, 5, 2, 6, 1, 7)
FAR_HEAD = (4, 5, 3, 2, 6, 7, 1)
LANES = 128


def rotary_tables():
    half = DIM // 2
    freq = (ROPE_BASE ** (-(np.arange(half) * 2.0 / DIM))).astype(np.float32).astype(np.float64)
    starts = np.arange(NX * NZ * TOKENS // LANES, dtype=np.float64) * LANES
    coarse = freq[:, None] * starts[None, :]
    coarse = coarse.reshape(half, -1, LANES).transpose(1, 0, 2)
    fine = freq[:, None] * np.arange(LANES, dtype=np.float64)[None, :]
    pair = lambda a, axis: np.stack([np.cos(a), np.sin(a)], axis=axis).astype(np.float32)
    row = np.concatenate([freq, freq]).astype(np.float32)[None, :]
    coarse = pair(coarse, 1).reshape(-1, half, LANES)
    return np.concatenate([coarse, pair(fine, 0), np.broadcast_to(row, (1, half, DIM))], axis=0)


def three(x):
    hi = x.astype(BF16).astype(F32)
    rest = x - hi
    mid = rest.astype(BF16).astype(F32)
    return hi, mid, rest - mid


def two(x):
    hi = x.astype(BF16).astype(F32)
    return hi, x - hi


def stack_rows(rows):
    sub = lax.broadcasted_iota(jnp.int32, (8, LANES), 0)
    out = jnp.zeros((8, LANES), F32)
    for index, row in enumerate(rows):
        out = jnp.where(sub == index, row, out)
    return out


def top_of(stats):
    return stats[0:1] + stats[1:2] + stats[2:3]


def total_of(stats):
    return stats[3:4] + stats[4:5]


def join(stats):
    tops = [top_of(s) for s in stats]
    peak = functools.reduce(jnp.maximum, tops)
    factors = [jnp.exp(t - peak) for t in tops]
    total = functools.reduce(jnp.add, [f * total_of(s) for f, s in zip(factors, stats)])
    return peak, total, factors


def kernel(
    q_hbm, kl_hbm, vl_hbm, ku_hbm, vu_hbm, w_hbm, prior_hbm, len_hbm, pos_hbm, table_hbm,
    out_ref, ev_ref,
    q_v, kl_v, vl_v, ku_v, vu_v, w_v, prior_v, len_ref, pos_i, coarse, fine,
    qa, keys, values, pos_v, score_a, score_b, weights, stat_v,
    xw, xr, zw, zr, ft, ax, acc, hw, hr,
    load_sem, xs_sem, xr_sem, zs_sem, zr_sem, as_sem, ar_sem, bs_sem, br_sem,
    hs_sem, hr_sem,
):
    ctx = lax.axis_index("ctx")
    head = lax.axis_index("head")
    z = ctx // NX
    x = lax.rem(ctx, NX)

    middle = TOKENS // 2
    table = lax.div(ctx, LANES * LANES // TOKENS) * 2
    moves = [
        ("ku", ku_hbm.at[0], ku_v),
        ("kl0", kl_hbm.at[0, 0:middle], kl_v.at[0:middle]),
        ("coarse", table_hbm.at[pl.ds(table, 2)], coarse),
        ("fine", table_hbm.at[table_hbm.shape[0] - 3 :], fine),
        ("pos", pos_hbm, pos_i),
        ("len", len_hbm, len_ref),
        ("q", q_hbm, q_v),
        ("kl1", kl_hbm.at[0, middle:TOKENS], kl_v.at[middle:TOKENS]),
        ("vu", vu_hbm.at[0], vu_v),
        ("vl", vl_hbm.at[0], vl_v),
        ("w", w_hbm, w_v),
        ("prior", prior_hbm, prior_v),
    ]

    def head_at(slot):
        if slot >= AWAY:
            return (slot - AWAY) * GROUP + x
        return slot // (NX - 1) * GROUP + lax.rem(x + FAR_X[slot % (NX - 1)], NX)

    loads = {}
    for i, (name, src, dst) in enumerate(moves):
        loads[name] = pltpu.make_async_copy(src, dst, load_sem.at[i])

    def begin(*names):
        for name in names:
            loads[name].start()

    begin("ku", "kl0", "coarse", "fine", "pos", "len", "kl1", "q", "vu", "vl", "w", "prior")

    def at_x(d):
        return {"ctx": z * NX + lax.rem(x + d, NX), "head": head}

    def at_z(d):
        return {"ctx": lax.rem(z + d, NZ) * NX + x, "head": head}

    def at_head(d):
        return {"ctx": ctx, "head": lax.rem(head + d, NHEAD)}

    peers = [at_x(d) for d in range(1, NX)] + [at_z(d) for d in range(1, NZ)] + [at_head(d) for d in range(1, NHEAD)]
    barrier = pltpu.get_barrier_semaphore()
    for peer in peers:
        pl.semaphore_signal(barrier, inc=1, device_id=peer, device_id_type=MESH)

    def send(src, dst, s_sem, r_sem, peer):
        copy = pltpu.make_async_remote_copy(
            src_ref=src, dst_ref=dst, send_sem=s_sem, recv_sem=r_sem, device_id=peer, device_id_type=MESH
        )
        copy.start()
        return copy

    pos_v[...] = jnp.zeros_like(pos_v)
    loads["pos"].wait()
    loads["fine"].wait()
    pos_v[0:STEPS, 0:ROWS] = pos_i[...].astype(F32)
    pos_t = jnp.transpose(pos_v[...])
    where_at = jnp.concatenate(
        [pos_t[8 * p : 8 * p + 8, s : s + 1] for p in range(NZ) for s in range(STEPS)], axis=0
    )
    angle = where_at * fine[2, 0:1, :]
    lane = lax.broadcasted_iota(jnp.int32, (HROWS, DIM), 1)
    cos_q = jnp.cos(angle)
    sin_q = jnp.where(lane < DIM // 2, -jnp.sin(angle), jnp.sin(angle))
    row_step = jnp.concatenate(
        [jnp.full((8, DIM), s, jnp.int32) for p in range(NZ) for s in range(STEPS)], axis=0
    )
    marks = jnp.where(lane == row_step, 1.0, 0.0).astype(BF16)

    half = DIM // 2
    token = ctx * TOKENS + lax.broadcasted_iota(jnp.int32, (16, TOKENS), 1)
    step_row = lax.broadcasted_iota(jnp.int32, (16, TOKENS), 0)
    loads["len"].wait()
    limit = jnp.where(step_row == 0, len_ref[0], jnp.where(step_row == 1, len_ref[1], len_ref[2]))
    dead = (step_row < STEPS) & (token >= limit)
    keys[DIM : DIM + 16, :] = jnp.where(dead, NEGATIVE, 0.0).astype(BF16)
    keys[DIM + 16 : 2 * DIM, :] = jnp.zeros((DIM - 16, TOKENS), BF16)
    loads["ku"].wait()
    key_up = jnp.transpose(ku_v[...].astype(F32)).astype(BF16)
    loads["coarse"].wait()
    shift = lax.rem(LANES - lax.rem(ctx, LANES * LANES // TOKENS) * (TOKENS // LANES), LANES)
    cos_c = pltpu.roll(coarse[0], shift, 1)
    sin_c = pltpu.roll(coarse[1], shift, 1)
    cos_f = fine[0]
    sin_f = fine[1]
    chunk = 512
    for start in range(0, TOKENS, chunk):
        if start == 0:
            loads["kl0"].wait()
        if start == middle:
            loads["kl1"].wait()
        raw = lax.dot_general(
            key_up, kl_v[start : start + chunk, :], (((1,), (1,)), ((), ())), preferred_element_type=F32
        )
        for off in range(0, chunk, LANES):
            a = (start + off) // LANES
            ca, sa = cos_c[:, a : a + 1], sin_c[:, a : a + 1]
            cosine = ca * cos_f - sa * sin_f
            sine = sa * cos_f + ca * sin_f
            first, second = raw[:half, off : off + LANES], raw[half:, off : off + LANES]
            keys[0:half, start + off : start + off + LANES] = (first * cosine - second * sine).astype(BF16)
            keys[half:DIM, start + off : start + off + LANES] = (second * cosine + first * sine).astype(BF16)

    def turn(u):
        for h in range(UNITS[u][0], sum(UNITS[u])):
            columns = pl.ds(pl.multiple_of(head_at(h) * DIM, DIM), DIM)
            block = [q_v[s, :, columns].astype(F32) for s in range(STEPS)]
            rows = jnp.concatenate([block[s][8 * p : 8 * p + 8] for p in range(NZ) for s in range(STEPS)], axis=0)
            turned = (rows * cos_q + pltpu.roll(rows, half, 1) * sin_q) * (DIM**-0.5)
            qa[h * HROWS : (h + 1) * HROWS, 0:DIM] = turned.astype(BF16)
            qa[h * HROWS : (h + 1) * HROWS, DIM : 2 * DIM] = marks

    loads["q"].wait()
    turn(0)

    def rows_of(u):
        return slice(UNITS[u][0] * HROWS, sum(UNITS[u]) * HROWS)

    def scores(u, dst):
        dst[0 : UNITS[u][1] * HROWS, :] = jnp.dot(qa[rows_of(u), :], keys[...], preferred_element_type=F32)

    stat_lane = lax.broadcasted_iota(jnp.int32, (HROWS, LANES), 1)
    filler = jnp.where(lax.broadcasted_iota(jnp.int32, (8, LANES), 1) == 3, 1.0, 0.0)

    def soft(u, src):
        s = src[0 : UNITS[u][1] * HROWS, :]
        top = jnp.max(s, axis=1, keepdims=True)
        expo = jnp.exp(s - top)
        total = jnp.sum(expo, axis=1, keepdims=True)
        w = expo.astype(BF16)
        weights[rows_of(u), :] = w
        sums = jnp.dot(w, values[...], preferred_element_type=F32)
        for i in range(UNITS[u][1]):
            h = UNITS[u][0] + i
            rows = slice(i * HROWS, (i + 1) * HROWS)
            columns = jnp.zeros((HROWS, LANES), F32)
            for k, part in enumerate((*three(top[rows]), *two(total[rows]))):
                columns = jnp.where(stat_lane == k, part, columns)
            spread = []
            for p in range(NZ):
                spread += [columns[LIVE * p : LIVE * (p + 1)], filler]
            stats = jnp.transpose(jnp.concatenate(spread, axis=0))[0:8]
            stat_v[h] = stats
            whole = jnp.concatenate([sums[rows], stats[:, 0:LANES], stats[:, LANES:PAD]], axis=0)
            xw[h] = whole.astype(BF16)

    sent = []

    def send_x(slot):
        g, d = slot // (NX - 1), FAR_X[slot % (NX - 1)]
        sent.append(send(xw.at[slot], xr.at[g, d - 1], xs_sem.at[g, d - 1], xr_sem.at[g, d - 1], at_x(d)))

    def wait_for(dst, sem):
        pltpu.make_async_copy(dst, dst, sem).wait()

    def merge_x(g):
        for d in range(1, NX):
            wait_for(xr.at[g, d - 1], xr_sem.at[g, d - 1])
        shares = [xw[AWAY + g].astype(F32)] + [xr[g, c].astype(F32) for c in range(NX - 1)]
        by_row, stats = [], []
        for q in range(NZ // 4):
            peak, total, factors = join([s[HROWS + 8 * q : HROWS + 8 * q + 8] for s in shares])
            turned = jnp.transpose(stack_rows(factors))
            by_row += [turned[BLOCK * b : BLOCK * b + LIVE] for b in range(4)]
            stats.append(stack_rows((*three(peak), *two(total))))
        by_row = jnp.concatenate(by_row, axis=0)
        merged = functools.reduce(jnp.add, [s[:HROWS] * by_row[:, c : c + 1] for c, s in enumerate(shares)])
        blocks = []
        for p in range(NZ):
            blocks += [merged[LIVE * p : LIVE * (p + 1)], stats[p // 4]]
        zw[g] = jnp.concatenate(blocks, axis=0).astype(BF16)

    def send_z(g):
        for d in FAR_Z:
            there = lax.rem(z + d, NZ)
            src = zw.at[g, pl.ds(pl.multiple_of(there * BLOCK, BLOCK), BLOCK)]
            sent.append(send(src, zr.at[g, d - 1], zs_sem.at[g, d - 1], zr_sem.at[g, d - 1], at_z(d)))

    def mine_z():
        return pl.ds(pl.multiple_of(z * BLOCK, BLOCK), BLOCK)

    def merge_z(g):
        for d in range(1, NZ):
            wait_for(zr.at[g, d - 1], zr_sem.at[g, d - 1])
        pieces = [zw[g, mine_z(), :].astype(F32)] + [zr[g, i].astype(F32) for i in range(NZ - 1)]
        peak, total, factors = join([p[LIVE:] for p in pieces])
        scale = 1.0 / total
        ft[:, 0:8] = jnp.transpose(stack_rows([f * scale for f in factors]))
        by_row = ft[pl.ds(pl.multiple_of(lax.rem(z, 4) * BLOCK, BLOCK), LIVE), 0:8]
        merged = functools.reduce(jnp.add, [p[:LIVE] * by_row[:, c : c + 1] for c, p in enumerate(pieces)])
        stats = stack_rows((*three(peak), *two(total)))
        ax[g * GROUP + x, mine_z(), :] = jnp.concatenate([merged, stats], axis=0).astype(BF16)

    def share_z(g):
        here = ax.at[g * GROUP + x, mine_z()]
        for d in FAR_Z:
            sent.append(send(here, here, as_sem.at[g, d - 1], ar_sem.at[g, d - 1], at_z(d)))

    def share_x(g):
        for d in range(1, NZ):
            here = ax.at[g * GROUP + x, mine_z()]
            wait_for(here, ar_sem.at[g, d - 1])
        here = ax.at[g * GROUP + x]
        for d in FAR_X:
            sent.append(send(here, here, bs_sem.at[g, d - 1], br_sem.at[g, d - 1], at_x(d)))

    def gathered(g):
        for d in range(1, NX):
            here = ax.at[g * GROUP + x]
            wait_for(here, br_sem.at[g, d - 1])

    done = []

    def project(first, count):
        rows = jnp.concatenate([ax[first + i] for i in range(count)], axis=1)
        part = jnp.dot(rows, w_v[first * DIM : (first + count) * DIM, :], preferred_element_type=F32)
        acc[...] = acc[...] + part if done else part
        done.append(first)

    pick_r = lax.broadcasted_iota(jnp.int32, (PAD, HROWS), 0)
    pick_c = lax.broadcasted_iota(jnp.int32, (PAD, HROWS), 1)
    low = pick_r & (BLOCK - 1)
    pick = jnp.where((low < LIVE) & (pick_r - 8 * (pick_r >> 5) == pick_c), 1.0, 0.0).astype(BF16)
    slot = lax.broadcasted_iota(jnp.int32, (8, LANES), 1)

    tallied = []

    def evict(first, count):
        tally = jnp.zeros((16, TOKENS), F32)
        for slot_at in range(first, first + count):
            h = head_at(slot_at)
            sides = []
            for q in range(NZ // 4):
                stats = jnp.zeros((8, LANES), F32)
                for b in range(4):
                    p = 4 * q + b
                    whole = ax[h, BLOCK * p : BLOCK * (p + 1), :].astype(F32)
                    stats = jnp.where(slot >> 5 == b, whole[LIVE:], stats)
                own = top_of(stat_v[slot_at][:, q * LANES : (q + 1) * LANES])
                coeff = jnp.exp(own - top_of(stats)) / total_of(stats)
                sides.append(jnp.where((slot[0:1] & (BLOCK - 1)) < LIVE, coeff, 0.0))
            coeff = jnp.broadcast_to(jnp.concatenate(sides, axis=1), (16, PAD)).astype(BF16)
            coeff = jnp.dot(coeff, pick, preferred_element_type=F32).astype(BF16)
            tally = tally + jnp.dot(coeff, weights[slot_at * HROWS : (slot_at + 1) * HROWS, :], preferred_element_type=F32)
        ev_ref[...] = (ev_ref[...] if tallied else prior_v[...]) + tally[0:1]
        tallied.append(first)

    def drain():
        while sent:
            sent.pop(0).wait_send()

    scores(0, score_a)
    turn(1)
    loads["vu"].wait()
    loads["vl"].wait()
    values[...] = jnp.dot(vl_v[...], vu_v[...], preferred_element_type=F32).astype(BF16)
    for u in range(len(UNITS)):
        now, later = (score_a, score_b) if u % 2 == 0 else (score_b, score_a)
        if u + 2 < len(UNITS):
            turn(u + 2)
        if u + 1 < len(UNITS):
            scores(u + 1, later)
        soft(u, now)
        if u == 1:
            pl.semaphore_wait(barrier, len(peers))
        if u >= 1:
            for slot_at in range(0 if u == 1 else UNITS[u][0], min(sum(UNITS[u]), AWAY)):
                send_x(slot_at)
    for g in range(GROUPS):
        merge_x(g)
        send_z(g)
    loads["w"].wait()
    loads["prior"].wait()
    for g in range(GROUPS):
        merge_z(g)
        share_z(g)
    for g in range(GROUPS):
        share_x(g)
    drain()
    for g in range(GROUPS):
        gathered(g)
        project(g * GROUP, GROUP)
    hw[...] = acc[...].astype(BF16)
    for d in FAR_HEAD:
        there = lax.rem(head + d, NHEAD)
        src = hw.at[pl.ds(pl.multiple_of(there * BLOCK, BLOCK), BLOCK)]
        sent.append(send(src, hr.at[d - 1], hs_sem.at[d - 1], hr_sem.at[d - 1], at_head(d)))
    for g in range(GROUPS):
        evict(g * GROUP, GROUP)
    final = acc[pl.ds(pl.multiple_of(head * BLOCK, BLOCK), BLOCK), :]
    for d in range(1, NHEAD):
        wait_for(hr.at[d - 1], hr_sem.at[d - 1])
        final = final + hr[d - 1].astype(F32)
    for s in range(STEPS):
        out_ref[s] = final[8 * s : 8 * s + 8].astype(BF16)
    drain()


def finish(a_ref, b_ref, out_ref, ev_ref):
    out_ref[...] = a_ref[...]
    ev_ref[...] = b_ref[...]


def local(queries, key_latent, value_latent, key_up, value_up, out_weight, prior, lengths, positions):
    table = rotary_tables()
    vmem = pl.BlockSpec(memory_space=pltpu.VMEM)
    hbm = pl.BlockSpec(memory_space=pl.ANY)
    dma = pltpu.SemaphoreType.DMA
    shapes = (
        jax.ShapeDtypeStruct((STEPS, ROWS // NHEAD, WIDTH), BF16),
        jax.ShapeDtypeStruct((1, TOKENS), F32),
    )
    raw = pl.pallas_call(
        kernel,
        out_shape=shapes,
        in_specs=[hbm] * 10,
        out_specs=(vmem, vmem),
        scratch_shapes=[
            pltpu.VMEM((STEPS, ROWS, HEADS * DIM), BF16),
            pltpu.VMEM((TOKENS, RANK), BF16),
            pltpu.VMEM((TOKENS, RANK), BF16),
            pltpu.VMEM((RANK, DIM), BF16),
            pltpu.VMEM((RANK, DIM), BF16),
            pltpu.VMEM((HEADS * DIM, WIDTH), BF16),
            pltpu.VMEM((1, TOKENS), F32),
            pltpu.SMEM((STEPS,), jnp.int32),
            pltpu.VMEM((STEPS, ROWS), jnp.int32),
            pltpu.VMEM((2, DIM // 2, LANES), F32),
            pltpu.VMEM((3, DIM // 2, LANES), F32),
            pltpu.VMEM((HEADS * HROWS, 2 * DIM), BF16),
            pltpu.VMEM((2 * DIM, TOKENS), BF16),
            pltpu.VMEM((TOKENS, DIM), BF16),
            pltpu.VMEM((8, LANES), F32),
            pltpu.VMEM((MOST * HROWS, TOKENS), F32),
            pltpu.VMEM((MOST * HROWS, TOKENS), F32),
            pltpu.VMEM((HEADS * HROWS, TOKENS), BF16),
            pltpu.VMEM((HEADS, 8, PAD), F32),
            pltpu.VMEM((HEADS, WIRE, DIM), BF16),
            pltpu.VMEM((GROUPS, NX - 1, WIRE, DIM), BF16),
            pltpu.VMEM((GROUPS, PAD, DIM), BF16),
            pltpu.VMEM((GROUPS, NZ - 1, BLOCK, DIM), BF16),
            pltpu.VMEM((LANES, LANES), F32),
            pltpu.VMEM((HEADS, PAD, DIM), BF16),
            pltpu.VMEM((PAD, WIDTH), F32),
            pltpu.VMEM((PAD, WIDTH), BF16),
            pltpu.VMEM((NHEAD - 1, BLOCK, WIDTH), BF16),
            dma((12,)),
            dma((GROUPS, NX - 1)),
            dma((GROUPS, NX - 1)),
            dma((GROUPS, NZ - 1)),
            dma((GROUPS, NZ - 1)),
            dma((GROUPS, NZ - 1)),
            dma((GROUPS, NZ - 1)),
            dma((GROUPS, NX - 1)),
            dma((GROUPS, NX - 1)),
            dma((NHEAD - 1,)),
            dma((NHEAD - 1,)),
        ],
        compiler_params=pltpu.CompilerParams(
            collective_id=0, has_side_effects=True, vmem_limit_bytes=56 * 2**20
        ),
        cost_estimate=pl.CostEstimate(flops=3_500_000_000, bytes_accessed=5_000_000, transcendentals=5_000_000),
        name="decode_attention",
    )(
        queries, key_latent, value_latent, key_up, value_up, out_weight, prior, lengths, positions,
        jnp.asarray(table),
    )
    return pl.pallas_call(
        finish, out_shape=shapes, in_specs=[vmem, vmem], out_specs=(vmem, vmem), name="finish"
    )(*raw)


def solution(mesh):
    placed = (
        P(None, None, "head"),
        P("head", "ctx", None),
        P("head", "ctx", None),
        P("head", None, None),
        P("head", None, None),
        P("head", "ctx"),
        P("head", "ctx"),
        P(),
        P(),
    )
    return jax.shard_map(
        local,
        mesh=mesh,
        in_specs=placed,
        out_specs=(P(None, "head", "ctx"), P("head", "ctx")),
        check_vma=False,
    )
```

time: 51.2 us -> 47.1 us (0.920)
  local copies, waits for them, and re-layouts: 2.63 us -> 0 us
  Pallas kernels: 47.7 us -> 46.3 us
    unnamed x2 -> x0, local copies, waits for them, and re-layouts: 2.63 us -> none
    pallas_call x1 -> x2, Pallas kernels: 47.7 us -> 46.3 us  [the longest x1 45 us: local(): pl.pallas_call(kernel, out_shape=shapes, in_specs=[hbm] * 10, out_specs=(...]
where the time goes in v2:
time: 47.1 us; the launch traced here: 47 us
  Pallas kernels  46.3 us (98%)
  between operations  0.64 us (1%)
    pallas_call x1, Pallas kernels, local(): pl.pallas_call(kernel, out_shape=shapes, in_specs=[hbm] * 10, out_specs=(...  45 us
    pallas_call x1, Pallas kernels, local(): pl.pallas_call(finish, out_shape=shapes, in_specs=[vmem, vmem], out_specs...  1.34 us

profile of v2, /device:TPU:1, one launch (start us, length us, event | category | flops | bytes accessed | tf_op | source)
XLA Modules:
  0.0 47.0 jit_solution(10000541633789223490)
XLA Ops:
  0.6 45.0 %decode_attention.1 = (bf16[3,8,384]{2,1,0:T(8,128)(2,1)}, f32[1,2048]{1,0:T(1,128)}) custom-call(bf16[3,64,1536]{2,1,0:T(8,128)(2,1)} %q_hbm.1, bf16[1,2048,256]{2,1,0:T(8,128)(2,1)} %kl_hbm.1, bf16[1,2048,256]{2,1,0:T(8,128)(2,1)} %vl_hbm.1, bf16[1,256,128]{2,1,0:T(8,128)(2,1)} %ku_hbm.1, bf16[1,256,128]{2,1,0:T(8,128)(2,1)} %vu_hbm.1, ...), custom_call_target="tpu_custom_call" | custom-call | flops 3500000000 | bytes 5000000 | tf_op jit(solution)/shard_map/decode_attention/pallas_call | solution.py:414
  45.7 1.3 %finish.1 = (bf16[3,8,384]{2,1,0:T(8,128)(2,1)}, f32[1,2048]{1,0:T(1,128)}) custom-call(bf16[3,8,384]{2,1,0:T(8,128)(2,1)} %get-tuple-element.4.a_ref, f32[1,2048]{1,0:T(1,128)} %get-tuple-element.5.b_ref), custom_call_target="tpu_custom_call" | custom-call | tf_op jit(solution)/shard_map/finish/pallas_call | solution.py:469

commit v3 on v2

--- a/solution.py
+++ b/solution.py
@@ -86,10 +86,10 @@
 
 def kernel(
     q_hbm, kl_hbm, vl_hbm, ku_hbm, vu_hbm, w_hbm, prior_hbm, len_hbm, pos_hbm, table_hbm,
-    out_ref, ev_ref,
-    q_v, kl_v, vl_v, ku_v, vu_v, w_v, prior_v, len_ref, pos_i, coarse, fine,
+    parts, ev_hbm,
+    ev_ref, q_v, kl_v, vl_v, ku_v, vu_v, w_v, prior_v, len_ref, pos_i, coarse, fine,
     qa, keys, values, pos_v, score_a, score_b, weights, stat_v,
-    xw, xr, zw, zr, ft, ax, acc, hw, hr,
+    xw, xr, zw, zr, ft, ax, acc, hw,
     load_sem, xs_sem, xr_sem, zs_sem, zr_sem, as_sem, ar_sem, bs_sem, br_sem,
     hs_sem, hr_sem,
 ):
@@ -382,24 +382,33 @@
         gathered(g)
         project(g * GROUP, GROUP)
     hw[...] = acc[...].astype(BF16)
+
+    def product(owner):
+        return hw.at[pl.ds(pl.multiple_of(owner * BLOCK, BLOCK), BLOCK)]
+
     for d in FAR_HEAD:
-        there = lax.rem(head + d, NHEAD)
-        src = hw.at[pl.ds(pl.multiple_of(there * BLOCK, BLOCK), BLOCK)]
-        sent.append(send(src, hr.at[d - 1], hs_sem.at[d - 1], hr_sem.at[d - 1], at_head(d)))
+        src = product(lax.rem(head + d, NHEAD))
+        sent.append(send(src, parts.at[d], hs_sem.at[d - 1], hr_sem.at[d - 1], at_head(d)))
+    own = pltpu.make_async_copy(product(head), parts.at[0], load_sem.at[0])
+    own.start()
     for g in range(GROUPS):
         evict(g * GROUP, GROUP)
-    final = acc[pl.ds(pl.multiple_of(head * BLOCK, BLOCK), BLOCK), :]
+    tally = pltpu.make_async_copy(ev_ref, ev_hbm, load_sem.at[1])
+    tally.start()
+    drain()
+    own.wait()
+    tally.wait()
+    for d in FAR_HEAD[::-1]:
+        wait_for(parts.at[d], hr_sem.at[d - 1])
+
+
+def finish(parts, tally, out_ref, ev_ref):
+    ev_ref[...] = tally[...]
+    final = parts[0].astype(F32)
     for d in range(1, NHEAD):
-        wait_for(hr.at[d - 1], hr_sem.at[d - 1])
-        final = final + hr[d - 1].astype(F32)
+        final = final + parts[d].astype(F32)
     for s in range(STEPS):
         out_ref[s] = final[8 * s : 8 * s + 8].astype(BF16)
-    drain()
-
-
-def finish(a_ref, b_ref, out_ref, ev_ref):
-    out_ref[...] = a_ref[...]
-    ev_ref[...] = b_ref[...]
 
 
 def local(queries, key_latent, value_latent, key_up, value_up, out_weight, prior, lengths, positions):
@@ -413,10 +422,11 @@
     )
     raw = pl.pallas_call(
         kernel,
-        out_shape=shapes,
+        out_shape=(jax.ShapeDtypeStruct((NHEAD, BLOCK, WIDTH), BF16), shapes[1]),
         in_specs=[hbm] * 10,
-        out_specs=(vmem, vmem),
+        out_specs=(hbm, hbm),
         scratch_shapes=[
+            pltpu.VMEM((1, TOKENS), F32),
             pltpu.VMEM((STEPS, ROWS, HEADS * DIM), BF16),
             pltpu.VMEM((TOKENS, RANK), BF16),
             pltpu.VMEM((TOKENS, RANK), BF16),
@@ -444,7 +454,6 @@
             pltpu.VMEM((HEADS, PAD, DIM), BF16),
             pltpu.VMEM((PAD, WIDTH), F32),
             pltpu.VMEM((PAD, WIDTH), BF16),
-            pltpu.VMEM((NHEAD - 1, BLOCK, WIDTH), BF16),
             dma((12,)),
             dma((GROUPS, NX - 1)),
             dma((GROUPS, NX - 1)),

time: 47.1 us -> 46.5 us (0.987)
  Pallas kernels: 46.3 us -> 45.7 us
    pallas_call x1, Pallas kernels: 45 us -> 44.2 us  [local(): pl.pallas_call(kernel, out_shape=(jax.ShapeDtypeStruct((NHEAD, BLOCK, WID...]
where the time goes in v3:
time: 46.5 us; the launch traced here: 46.4 us
  Pallas kernels  45.7 us (98%)
  between operations  0.64 us (1%)
    pallas_call x1, Pallas kernels, local(): pl.pallas_call(kernel, out_shape=(jax.ShapeDtypeStruct((NHEAD, BLOCK, WID...  44.2 us
    pallas_call x1, Pallas kernels, local(): pl.pallas_call(finish, out_shape=shapes, in_specs=[vmem, vmem], out_specs...  1.56 us

profile of v3, /device:TPU:1, one launch (start us, length us, event | category | flops | bytes accessed | tf_op | source)
XLA Modules:
  0.0 46.4 jit_solution(5726561695387650349)
XLA Ops:
  0.6 44.2 %decode_attention.1 = (bf16[8,32,384]{2,1,0:T(8,128)(2,1)}, f32[1,2048]{1,0:T(1,128)}) custom-call(bf16[3,64,1536]{2,1,0:T(8,128)(2,1)} %q_hbm.1, bf16[1,2048,256]{2,1,0:T(8,128)(2,1)} %kl_hbm.1, bf16[1,2048,256]{2,1,0:T(8,128)(2,1)} %vl_hbm.1, bf16[1,256,128]{2,1,0:T(8,128)(2,1)} %ku_hbm.1, bf16[1,256,128]{2,1,0:T(8,128)(2,1)} %vu_hbm.1, ...), custom_call_target="tpu_custom_call" | custom-call | flops 3500000000 | bytes 5000000 | tf_op jit(solution)/shard_map/decode_attention/pallas_call | solution.py:423
  44.8 1.6 %finish.1 = (bf16[3,8,384]{2,1,0:T(8,128)(2,1)}, f32[1,2048]{1,0:T(1,128)}) custom-call(bf16[8,32,384]{2,1,0:T(8,128)(2,1)} %get-tuple-element.4.parts, f32[1,2048]{1,0:T(1,128)} %get-tuple-element.5.tally), custom_call_target="tpu_custom_call" | custom-call | tf_op jit(solution)/shard_map/finish/pallas_call | solution.py:478

commit v4 on v3

--- a/solution.py
+++ b/solution.py
@@ -23,10 +23,10 @@
 BLOCK = LIVE + 8
 PAD = NZ * BLOCK
 HROWS = STEPS * ROWS
-MOST = 3
+MOST = 1
 GROUP = NX
 GROUPS = HEADS // GROUP
-UNITS = ((0, 2), (2, 2), (4, 2), (6, 2), (8, 1), (9, 1), (10, 1), (11, 1))
+UNITS = tuple((slot, 1) for slot in range(HEADS))
 WIRE = HROWS + 16
 FAR_X = (2, 1, 3)
 AWAY = GROUPS * (NX - 1)

time: 46.5 us -> 45.7 us (0.983)
  Pallas kernels: 45.7 us -> 45 us
    pallas_call x1, Pallas kernels: 44.2 us -> 43.4 us  [local(): pl.pallas_call(kernel, out_shape=(jax.ShapeDtypeStruct((NHEAD, BLOCK, WID...]
where the time goes in v4:
time: 45.7 us; the launch traced here: 45.6 us
  Pallas kernels  45 us (98%)
  between operations  0.64 us (1%)
    pallas_call x1, Pallas kernels, local(): pl.pallas_call(kernel, out_shape=(jax.ShapeDtypeStruct((NHEAD, BLOCK, WID...  43.4 us
    pallas_call x1, Pallas kernels, local(): pl.pallas_call(finish, out_shape=shapes, in_specs=[vmem, vmem], out_specs...  1.56 us

profile of v4, /device:TPU:1, one launch (start us, length us, event | category | flops | bytes accessed | tf_op | source)
XLA Modules:
  0.0 45.6 jit_solution(5775617846158040455)
XLA Ops:
  0.6 43.4 %decode_attention.1 = (bf16[8,32,384]{2,1,0:T(8,128)(2,1)}, f32[1,2048]{1,0:T(1,128)}) custom-call(bf16[3,64,1536]{2,1,0:T(8,128)(2,1)} %q_hbm.1, bf16[1,2048,256]{2,1,0:T(8,128)(2,1)} %kl_hbm.1, bf16[1,2048,256]{2,1,0:T(8,128)(2,1)} %vl_hbm.1, bf16[1,256,128]{2,1,0:T(8,128)(2,1)} %ku_hbm.1, bf16[1,256,128]{2,1,0:T(8,128)(2,1)} %vu_hbm.1, ...), custom_call_target="tpu_custom_call" | custom-call | flops 3500000000 | bytes 5000000 | tf_op jit(solution)/shard_map/decode_attention/pallas_call | solution.py:423
  44.0 1.6 %finish.1 = (bf16[3,8,384]{2,1,0:T(8,128)(2,1)}, f32[1,2048]{1,0:T(1,128)}) custom-call(bf16[8,32,384]{2,1,0:T(8,128)(2,1)} %get-tuple-element.4.parts, f32[1,2048]{1,0:T(1,128)} %get-tuple-element.5.tally), custom_call_target="tpu_custom_call" | custom-call | tf_op jit(solution)/shard_map/finish/pallas_call | solution.py:478

commit v5 on v4

--- a/solution.py
+++ b/solution.py
@@ -377,7 +377,6 @@
         share_z(g)
     for g in range(GROUPS):
         share_x(g)
-    drain()
     for g in range(GROUPS):
         gathered(g)
         project(g * GROUP, GROUP)

time: 45.7 us -> 45.7 us (level)
  no operation moved by 1% of the time
where the time goes in v5:
time: 45.7 us; the launch traced here: 45.6 us
  Pallas kernels  45 us (98%)
  between operations  0.64 us (1%)
    pallas_call x1, Pallas kernels, local(): pl.pallas_call(kernel, out_shape=(jax.ShapeDtypeStruct((NHEAD, BLOCK, WID...  43.4 us
    pallas_call x1, Pallas kernels, local(): pl.pallas_call(finish, out_shape=shapes, in_specs=[vmem, vmem], out_specs...  1.56 us

profile of v5, /device:TPU:1, one launch (start us, length us, event | category | flops | bytes accessed | tf_op | source)
XLA Modules:
  0.0 45.6 jit_solution(479820289868953582)
XLA Ops:
  0.6 43.4 %decode_attention.1 = (bf16[8,32,384]{2,1,0:T(8,128)(2,1)}, f32[1,2048]{1,0:T(1,128)}) custom-call(bf16[3,64,1536]{2,1,0:T(8,128)(2,1)} %q_hbm.1, bf16[1,2048,256]{2,1,0:T(8,128)(2,1)} %kl_hbm.1, bf16[1,2048,256]{2,1,0:T(8,128)(2,1)} %vl_hbm.1, bf16[1,256,128]{2,1,0:T(8,128)(2,1)} %ku_hbm.1, bf16[1,256,128]{2,1,0:T(8,128)(2,1)} %vu_hbm.1, ...), custom_call_target="tpu_custom_call" | custom-call | flops 3500000000 | bytes 5000000 | tf_op jit(solution)/shard_map/decode_attention/pallas_call | solution.py:422
  44.0 1.6 %finish.1 = (bf16[3,8,384]{2,1,0:T(8,128)(2,1)}, f32[1,2048]{1,0:T(1,128)}) custom-call(bf16[8,32,384]{2,1,0:T(8,128)(2,1)} %get-tuple-element.4.parts, f32[1,2048]{1,0:T(1,128)} %get-tuple-element.5.tally), custom_call_target="tpu_custom_call" | custom-call | tf_op jit(solution)/shard_map/finish/pallas_call | solution.py:477
